TPU v7x, 256 devices: a whole 4x4x8 slice. The times are simulated.
256 devices in a mesh: dp: 16 (over x, z_lo), expert: 16 (over z_hi, y, core).
Axes of the slice: x: 4, y: 4, z: 8 (z_hi: 2, z_lo: 4; z = z_hi * 4 + z_lo), core: 2. Of those that a mesh axis runs over, the one named last changes fastest.
Arguments:
- tokens: bfloat16 [8192, 4096], P('expert', 'dp'), may hold values from -6 to 6
- expert_ids: int32 [8192, 2], P('expert'), may hold values from 0 to 31, all different within a row; in each aligned block of 512 rows (0 to 511, 512 to 1023, ...) at most 64 rows name the same one
- gate_values: float32 [8192, 2], P('expert'), may hold values from 0.2 to 1
- w_in: bfloat16 [32, 4096, 1536], P('expert', 'dp'), may hold values from -0.09375 to 0.09375
- w_out: bfloat16 [32, 1536, 4096], P('expert', None, 'dp'), may hold values from -0.15625 to 0.15625
- grad_out: bfloat16 [8192, 4096], P('expert', 'dp'), may hold values from -3 to 3
Outputs:
- mixed: bfloat16 [8192, 4096], P('expert', 'dp')
- grad_tokens: bfloat16 [8192, 4096], P('expert', 'dp')
- grad_w_in: float32 [32, 4096, 1536], P('expert', 'dp')
- grad_w_out: float32 [32, 1536, 4096], P('expert', None, 'dp')
Inputs may be any that keep to these rules, and one draw needn't show every extreme that they name: `expert_ids`: each row names 2 different experts; among the 512 rows of one index of expert no expert is named by more than 64 rows, a bound that some block reaches.
All inputs are finite; a program needn't handle non-finite values.
Results may differ from a plain program's by a relative error of at most 0.03.
Values may be sent and summed in bfloat16 or wider, within the bound.
A program may use at most 128 MiB of HBM per device.

v0:
```python
import jax
import jax.numpy as jnp
from jax import lax
from jax.sharding import PartitionSpec as P

TOP = 2
EXP_DEV = 2


def gelu_value(pre):
    return jax.nn.gelu(pre, approximate=True)


def gelu_slope(pre):
    value, pullback = jax.vjp(gelu_value, pre)
    return pullback(jnp.ones_like(pre))[0]


def slot_index(expert_ids, num_experts, capacity):
    flat = expert_ids.reshape(-1)
    onehot = (flat[:, None] == jnp.arange(num_experts, dtype=jnp.int32)[None, :]).astype(jnp.int32)
    before = jnp.cumsum(onehot, axis=0) - onehot
    position = jnp.sum(before * onehot, axis=1)
    return flat * capacity + position


def sum_apart(partial_value):
    return lax.psum_scatter(
        partial_value.astype(jnp.bfloat16), "dp", scatter_dimension=0, tiled=True
    ).astype(jnp.float32)


def gather_apart(share):
    return lax.all_gather(share, "dp", axis=0, tiled=True)


def send_back(slot_rows):
    return lax.all_to_all(slot_rows, "expert", split_axis=0, concat_axis=0, tiled=True)


def body(tokens, expert_ids, gate_values, w_in, w_out, grad_out):
    groups = lax.axis_size("expert")
    tok_rows = tokens.shape[0]
    width = tokens.shape[1]
    hidden = w_in.shape[2]
    num_experts = EXP_DEV * groups
    capacity = 2 * tok_rows * TOP // num_experts
    total = num_experts * capacity
    slots = slot_index(expert_ids, num_experts, capacity)
    pair_rows = jnp.repeat(tokens, TOP, axis=0)
    scaled = (
        (gate_values[:, :, None] * grad_out[:, None, :].astype(jnp.float32))
        .astype(jnp.bfloat16)
        .reshape(tok_rows * TOP, width)
    )
    send_rows = (
        jnp.zeros((total, width), jnp.bfloat16)
        .at[slots]
        .set(pair_rows)
        .reshape(groups, EXP_DEV * capacity, width)
    )
    send_grads = (
        jnp.zeros((total, width), jnp.bfloat16)
        .at[slots]
        .set(scaled)
        .reshape(groups, EXP_DEV * capacity, width)
    )

    def inbound(rows):
        return rows.reshape(groups, EXP_DEV, capacity, width)

    got_rows = inbound(lax.all_to_all(send_rows, "expert", split_axis=0, concat_axis=0, tiled=True))
    pre_share = sum_apart(
        jnp.einsum("slcd,ldh->slch", got_rows, w_in, preferred_element_type=jnp.float32).reshape(
            -1, hidden
        )
    )
    act = gather_apart(gelu_value(pre_share).astype(jnp.bfloat16)).reshape(
        groups, EXP_DEV, capacity, hidden
    )
    result = jnp.einsum("slch,lhd->slcd", act, w_out, preferred_element_type=jnp.float32).astype(
        jnp.bfloat16
    )
    arrived = send_back(result.reshape(groups, EXP_DEV * capacity, width)).reshape(total, width)
    picked = arrived[slots].reshape(tok_rows, TOP, width).astype(jnp.float32)
    mixed = jnp.sum(gate_values[:, :, None] * picked, axis=1).astype(jnp.bfloat16)
    got_grads = inbound(
        lax.all_to_all(send_grads, "expert", split_axis=0, concat_axis=0, tiled=True)
    )
    slope_share = sum_apart(
        jnp.einsum("slcd,lhd->slch", got_grads, w_out, preferred_element_type=jnp.float32).reshape(
            -1, hidden
        )
    )
    delta = gather_apart((slope_share * gelu_slope(pre_share)).astype(jnp.bfloat16)).reshape(
        groups, EXP_DEV, capacity, hidden
    )
    grad_w_out = jnp.einsum("slch,slcd->lhd", act, got_grads, preferred_element_type=jnp.float32)
    grad_w_in = jnp.einsum("slcd,slch->ldh", got_rows, delta, preferred_element_type=jnp.float32)
    back = jnp.einsum("slch,ldh->slcd", delta, w_in, preferred_element_type=jnp.float32).astype(
        jnp.bfloat16
    )
    returned = send_back(back.reshape(groups, EXP_DEV * capacity, width)).reshape(total, width)
    gathered = returned[slots].reshape(tok_rows, TOP, width).astype(jnp.float32)
    grad_tokens = jnp.sum(gathered, axis=1).astype(jnp.bfloat16)
    return (mixed, grad_tokens, grad_w_in, grad_w_out)


def solution(mesh):
    return jax.shard_map(
        body,
        mesh=mesh,
        in_specs=(
            P("expert", "dp"),
            P("expert", None),
            P("expert", None),
            P("expert", "dp", None),
            P("expert", None, "dp"),
            P("expert", "dp"),
        ),
        out_specs=(
            P("expert", "dp"),
            P("expert", "dp"),
            P("expert", "dp", None),
            P("expert", None, "dp"),
        ),
        check_vma=False,
    )
```

profile of v0, /device:TPU:1, one launch (start us, length us, event | category | flops | bytes accessed | tf_op | source)
XLA Modules:
  0.0 750.2 jit_solution(10159270436512219492)
XLA Ops:
  9.2 9.0 %reduce-window.6 = s32[32,8,128]{2,1,0:T(8,128)S(1)} reduce-window(s32[32,8,128]{2,1,0:T(8,128)S(1)} %fusion.48, s32[]{:T(128)} %constant.6.clone.1), window={size=1x1x128 pad=0_0x0_0x127_0}, to_apply=%region_0.0 | reduce-window | flops 4161536 | bytes 262148 | tf_op jit(solution)/shard_map/reduce-window
  20.0 2.2 mul.101
  24.2 6.5 scatter_custom_fusion.1
  30.7 34.4 %all_to_all.20 = bf16[16,128,256]{2,1,0:T(8,128)(2,1)S(1)} all-to-all(bf16[16,128,256]{2,1,0:T(8,128)(2,1)} %bitcast.77), channel_id=1, replica_groups=mesh['dp'=16,'expert'=16] {'expert'}, dimensions={0} | all-to-all | bytes 2097152 | tf_op jit(solution)/shard_map/all_to_all | solution.py:88
  66.9 3.3 copy.23
  71.7 5.3 scatter_custom_fusion
  77.0 45.9 %all_to_all.21 = bf16[16,128,256]{2,1,0:T(8,128)(2,1)S(1)} all-to-all(bf16[16,128,256]{2,1,0:T(8,128)(2,1)S(1)} %bitcast.79), channel_id=1, replica_groups=mesh['dp'=16,'expert'=16] {'expert'}, dimensions={0} | all-to-all | bytes 2097152 | tf_op jit(solution)/shard_map/all_to_all | solution.py:72
  122.9 3.6 convert_bitcast_fusion.1
  126.5 3.3 copy.18
  129.9 113.1 %reduce-scatter.5.cloned.1.call-done = bf16[128,1536]{1,0:T(8,128)(2,1)} async-done(((bf16[2048,1536]{1,0:T(8,128)(2,1)}), bf16[128,1536]{1,0:T(8,128)(2,1)}) %reduce-scatter.5.cloned.1.call-update) | async-done | bytes 393232 | tf_op jit(solution)/shard_map/reduce_scatter | solution.py:28
  243.0 141.9 %reduce-scatter.3.cloned.1.call-done = bf16[128,1536]{1,0:T(8,128)(2,1)} async-done(((bf16[2048,1536]{1,0:T(8,128)(2,1)}), bf16[128,1536]{1,0:T(8,128)(2,1)}) %reduce-scatter.3.cloned.1.call-update) | async-done | bytes 393232 | tf_op jit(solution)/shard_map/reduce_scatter | solution.py:28
  385.0 2.6 fusion.34
  388.1 140.9 %all-gather.3.cloned.1.call-done = bf16[2048,1536]{1,0:T(8,128)(2,1)} async-done(((bf16[128,1536]{1,0:T(8,128)(2,1)}), bf16[2048,1536]{1,0:T(8,128)(2,1)}) %all-gather.3.cloned.1.call-update) | async-done | bytes 6291472 | tf_op jit(solution)/shard_map/all_gather | solution.py:34
  529.0 4.6 fusion.23
  534.6 7.7 %all-to-all-start.1 = ((bf16[16,128,256]{2,1,0:T(8,128)(2,1)}), bf16[16,128,256]{2,1,0:T(8,128)(2,1)S(1)}, u32[]{:S(2)}, u32[]{:S(2)}) async-start(bf16[16,128,256]{2,1,0:T(8,128)(2,1)} %bitcast.14), calls=%async_computation.2 | async-start | bytes 2097152 | tf_op jit(solution)/shard_map/all_to_all | solution.py:38
  542.3 152.2 %all-gather.5.cloned.1.call-done = bf16[2048,1536]{1,0:T(8,128)(2,1)} async-done(((bf16[128,1536]{1,0:T(8,128)(2,1)}), bf16[2048,1536]{1,0:T(8,128)(2,1)}) %all-gather.5.cloned.1.call-update) | async-done | bytes 6291472 | tf_op jit(solution)/shard_map/all_gather | solution.py:34
  694.5 5.1 fusion.18
  700.7 7.7 %all-to-all-start.3 = ((bf16[16,128,256]{2,1,0:T(8,128)(2,1)}), bf16[16,128,256]{2,1,0:T(8,128)(2,1)}, u32[]{:S(2)}, u32[]{:S(2)}) async-start(bf16[16,128,256]{2,1,0:T(8,128)(2,1)} %bitcast.78), calls=%async_computation.5 | async-start | bytes 2097152 | tf_op jit(solution)/shard_map/all_to_all | solution.py:38
  708.4 7.1 convolution_bitcast_fusion
  715.5 6.3 convolution_bitcast_fusion.1
  721.8 3.9 gather_fusion
  726.2 3.6 multiply_reduce_fusion
  729.8 6.7 all-to-all-done.3
  736.5 4.8 gather_fusion.1
  (50 shorter events, 14.6 us)
Async XLA Ops:
  7.2 57.9 %copy-start = (bf16[2,1536,256]{2,1,0:T(8,128)(2,1)S(1)}, bf16[2,1536,256]{2,1,0:T(8,128)(2,1)}, u32[]{:S(2)}) copy-start(bf16[2,1536,256]{2,1,0:T(8,128)(2,1)} %param.10) | copy-start | bytes 4718596
  7.2 235.9 %reduce-scatter.5.cloned.1.call-start = ((), (), s32[]{:S(2)}) async-start(), calls=%async_computation.8 | async-start | bytes 6684672 | tf_op jit(solution)/shard_map/reduce_scatter | solution.py:28
  65.1 5.2 copy-start.2
  70.3 1.0 copy-start.6
  70.3 314.7 %reduce-scatter.3.cloned.1.call-start = ((), (), s32[]{:S(2)}) async-start(), calls=%async_computation.6 | async-start | bytes 6684672 | tf_op jit(solution)/shard_map/reduce_scatter | solution.py:28
  122.9 6.9 copy-start.4
  129.9 399.1 %all-gather.3.cloned.1.call-start = ((), (), s32[]{:S(2)}) async-start(), calls=%async_computation.7 | async-start | bytes 6684672 | tf_op jit(solution)/shard_map/all_gather | solution.py:34
  387.5 306.9 %all-gather.5.cloned.1.call-start = ((), (), s32[]{:S(2)}) async-start(), calls=%async_computation.9 | async-start | bytes 6684672 | tf_op jit(solution)/shard_map/all_gather | solution.py:34
  534.6 166.1 %all-to-all-start.1 = ((bf16[16,128,256]{2,1,0:T(8,128)(2,1)}), bf16[16,128,256]{2,1,0:T(8,128)(2,1)S(1)}, u32[]{:S(2)}, u32[]{:S(2)}) async-start(bf16[16,128,256]{2,1,0:T(8,128)(2,1)} %bitcast.14), calls=%async_computation.2 | async-start | bytes 2097152 | tf_op jit(solution)/shard_map/all_to_all | solution.py:38
  694.5 13.9 %copy-start.3 = (bf16[16,128,256]{2,1,0:T(8,128)(2,1)S(1)}, bf16[16,128,256]{2,1,0:T(8,128)(2,1)}, u32[]{:S(2)}) copy-start(bf16[16,128,256]{2,1,0:T(8,128)(2,1)} %copy-done.2) | copy-start | bytes 3145732
  700.7 35.8 %all-to-all-start.3 = ((bf16[16,128,256]{2,1,0:T(8,128)(2,1)}), bf16[16,128,256]{2,1,0:T(8,128)(2,1)}, u32[]{:S(2)}, u32[]{:S(2)}) async-start(bf16[16,128,256]{2,1,0:T(8,128)(2,1)} %bitcast.78), calls=%async_computation.5 | async-start | bytes 2097152 | tf_op jit(solution)/shard_map/all_to_all | solution.py:38
  708.4 7.1 copy-start.5
  721.8 21.9 %copy-start.1 = (bf16[2,1536,256]{2,1,0:T(8,128)(2,1)S(1)}, bf16[2,1536,256]{2,1,0:T(8,128)(2,1)}, u32[]{:S(2)}) copy-start(bf16[2,1536,256]{2,1,0:T(8,128)(2,1)} %param.10) | copy-start | bytes 4718596
Sparse Core Ops, SparseCore 0:
  70.4 172.5 reduce-scatter.4
  245.6 139.3 reduce-scatter.2
  387.7 141.2 all-gather.2
  530.6 163.7 all-gather.4
where the time goes:
time: 751 us; the launch traced here: 750 us
  waiting for transfers between devices  555 us (74%)
  blocking collectives  80.3 us (11%)
  local copies, waits for them, and re-layouts  32 us (4%)
  matrix products  28.5 us (4%)
  other arithmetic  24.6 us (3%)
  starting transfers between devices  15.5 us (2%)
  between operations  14 us (2%)
    all_gather x2, waiting for transfers between devices, gather_apart(): return lax.all_gather(share, 'dp', axis=0, tiled=True)  293 us
    reduce_scatter x2, waiting for transfers between devices, sum_apart(): lax.psum_scatter(partial_value.astype(jnp.bfloat16), 'dp', scatter_dimens...  255 us
    all_to_all x1, blocking collectives, body(): lax.all_to_all(send_rows, 'expert', split_axis=0, concat_axis=0, tiled=True)  45.9 us
    all_to_all x1, blocking collectives, body(): lax.all_to_all(send_grads, 'expert', split_axis=0, concat_axis=0, tiled=T...  34.4 us
    all_to_all x2, starting transfers between devices, send_back(): lax.all_to_all(slot_rows, 'expert', split_axis=0, concat_axis=0, tiled=True)  15.3 us
  transfers between devices with their start and end apart: 6, of which 5 were waited for; matrix products, arithmetic and copies ran while one was open for 6% of the time, Pallas kernels for 0%

commit v1 on v0

--- a/solution.py
+++ b/solution.py
@@ -5,6 +5,11 @@
 
 TOP = 2
 EXP_DEV = 2
+
+
+def gather_over(array, axis, dim):
+    sent = jnp.stack([array] * lax.axis_size(axis))
+    return jnp.concatenate(lax.all_to_all(sent, axis, 0, 0), axis=dim)
 
 
 def gelu_value(pre):
@@ -31,7 +36,7 @@
 
 
 def gather_apart(share):
-    return lax.all_gather(share, "dp", axis=0, tiled=True)
+    return gather_over(share, "dp", 0)
 
 
 def send_back(slot_rows):

time: 751 us -> 763 us (1.016)
  waiting for transfers between devices: 555 us -> 411 us
  blocking collectives: 80.3 us -> 223 us
    all_gather x2 -> x0, waiting for transfers between devices: 293 us -> none  [gather_apart(): return lax.all_gather(share, 'dp', axis=0, tiled=True)]
    all_to_all x0 -> x1, blocking collectives: none -> 143 us  [gather_over(): return jnp.concatenate(lax.all_to_all(sent, axis, 0, 0), axis=dim)]
    all_to_all x0 -> x1, waiting for transfers between devices: none -> 135 us  [gather_over(): return jnp.concatenate(lax.all_to_all(sent, axis, 0, 0), axis=dim)]
    all_to_all x2, waiting for transfers between devices: 6.72 us -> 21.3 us  [send_back(): lax.all_to_all(slot_rows, 'expert', split_axis=0, concat_axis=0, tiled=True)]
  transfers between devices with their start and end apart: 6 -> 5, of which waited for: 5 -> 4; matrix products, arithmetic and copies ran while one was open for 6% -> 6% of each run, Pallas kernels for 0% -> 0%
where the time goes in v1:
time: 763 us; the launch traced here: 760 us
  waiting for transfers between devices  411 us (54%)
  blocking collectives  223 us (29%)
  local copies, waits for them, and re-layouts  37.7 us (5%)
  matrix products  28.3 us (4%)
  other arithmetic  23.7 us (3%)
  starting transfers between devices  22.5 us (3%)
  between operations  14.2 us (2%)
    reduce_scatter x2, waiting for transfers between devices, sum_apart(): lax.psum_scatter(partial_value.astype(jnp.bfloat16), 'dp', scatter_dimens...  254 us
    all_to_all x1, blocking collectives, gather_over(): return jnp.concatenate(lax.all_to_all(sent, axis, 0, 0), axis=dim)  143 us
    all_to_all x1, waiting for transfers between devices, gather_over(): return jnp.concatenate(lax.all_to_all(sent, axis, 0, 0), axis=dim)  135 us
    all_to_all x1, blocking collectives, body(): lax.all_to_all(send_rows, 'expert', split_axis=0, concat_axis=0, tiled=True)  45.9 us
    all_to_all x1, blocking collectives, body(): lax.all_to_all(send_grads, 'expert', split_axis=0, concat_axis=0, tiled=T...  34.4 us
    all_to_all x2, waiting for transfers between devices, send_back(): lax.all_to_all(slot_rows, 'expert', split_axis=0, concat_axis=0, tiled=True)  21.3 us
    all_to_all x2, starting transfers between devices, send_back(): lax.all_to_all(slot_rows, 'expert', split_axis=0, concat_axis=0, tiled=True)  17.7 us
  transfers between devices with their start and end apart: 5, of which 4 were waited for; matrix products, arithmetic and copies ran while one was open for 6% of the time, Pallas kernels for 0%

profile of v1, /device:TPU:1, one launch (start us, length us, event | category | flops | bytes accessed | tf_op | source)
XLA Modules:
  0.0 760.4 jit_solution(5482359741221395750)
XLA Ops:
  9.2 9.0 %reduce-window.6 = s32[32,8,128]{2,1,0:T(8,128)S(1)} reduce-window(s32[32,8,128]{2,1,0:T(8,128)S(1)} %fusion.48, s32[]{:T(128)} %constant.6.clone.1), window={size=1x1x128 pad=0_0x0_0x127_0}, to_apply=%region_0.0 | reduce-window | flops 4161536 | bytes 262148 | tf_op jit(solution)/shard_map/reduce-window
  24.2 6.5 scatter_custom_fusion.1
  30.7 34.4 %all_to_all.30 = bf16[16,128,256]{2,1,0:T(8,128)(2,1)S(1)} all-to-all(bf16[16,128,256]{2,1,0:T(8,128)(2,1)} %bitcast.79), channel_id=1, replica_groups=mesh['dp'=16,'expert'=16] {'expert'}, dimensions={0} | all-to-all | bytes 2097152 | tf_op jit(solution)/shard_map/all_to_all | solution.py:93
  67.9 3.3 copy.23
  72.7 5.3 scatter_custom_fusion
  78.0 45.9 %all_to_all.31 = bf16[16,128,256]{2,1,0:T(8,128)(2,1)S(1)} all-to-all(bf16[16,128,256]{2,1,0:T(8,128)(2,1)S(1)} %bitcast.82), channel_id=1, replica_groups=mesh['dp'=16,'expert'=16] {'expert'}, dimensions={0} | all-to-all | bytes 2097152 | tf_op jit(solution)/shard_map/all_to_all | solution.py:77
  124.9 3.2 convert_bitcast_fusion.1
  128.1 3.3 copy.18
  131.4 112.6 %reduce-scatter.5.cloned.1.call-done = bf16[128,1536]{1,0:T(8,128)(2,1)} async-done(((bf16[2048,1536]{1,0:T(8,128)(2,1)}), bf16[128,1536]{1,0:T(8,128)(2,1)}) %reduce-scatter.5.cloned.1.call-update) | async-done | bytes 393232 | tf_op jit(solution)/shard_map/reduce_scatter | solution.py:33
  244.0 141.9 %reduce-scatter.3.cloned.1.call-done = bf16[128,1536]{1,0:T(8,128)(2,1)} async-done(((bf16[2048,1536]{1,0:T(8,128)(2,1)}), bf16[128,1536]{1,0:T(8,128)(2,1)}) %reduce-scatter.3.cloned.1.call-update) | async-done | bytes 393232 | tf_op jit(solution)/shard_map/reduce_scatter | solution.py:33
  388.3 142.7 %all_to_all.32 = bf16[16,128,1536]{2,1,0:T(8,128)(2,1)} all-to-all(bf16[16,128,1536]{2,1,0:T(8,128)(2,1)S(1)} %stack.4), channel_id=1, replica_groups=mesh['dp'=16,'expert'=16] {'dp'}, dimensions={0} | all-to-all | bytes 12582912 | tf_op jit(solution)/shard_map/all_to_all | solution.py:12
  531.0 3.2 stack.5
  534.2 4.7 all-to-all-start.4
  538.9 4.6 fusion.23
  544.5 135.1 %all-to-all-done.4 = bf16[16,128,1536]{2,1,0:T(8,128)(2,1)} async-done(((bf16[16,128,1536]{2,1,0:T(8,128)(2,1)}), bf16[16,128,1536]{2,1,0:T(8,128)(2,1)}, u32[]{:S(2)}, u32[]{:S(2)}) %all-to-all-start.4) | async-done | bytes 6291488 | tf_op jit(solution)/shard_map/all_to_all | solution.py:12
  679.6 10.8 %all-to-all-start.2 = ((bf16[16,128,256]{2,1,0:T(8,128)(2,1)}), bf16[16,128,256]{2,1,0:T(8,128)(2,1)S(1)}, u32[]{:S(2)}, u32[]{:S(2)}) async-start(bf16[16,128,256]{2,1,0:T(8,128)(2,1)} %bitcast.81), calls=%async_computation.3 | async-start | bytes 2097152 | tf_op jit(solution)/shard_map/all_to_all | solution.py:43
  690.4 5.0 fusion.18
  696.5 21.3 %all-to-all-done.2 = bf16[16,128,256]{2,1,0:T(8,128)(2,1)S(1)} async-done(((bf16[16,128,256]{2,1,0:T(8,128)(2,1)}), bf16[16,128,256]{2,1,0:T(8,128)(2,1)S(1)}, u32[]{:S(2)}, u32[]{:S(2)}) %all-to-all-start.2) | async-done | bytes 1048608 | tf_op jit(solution)/shard_map/all_to_all | solution.py:43
  717.9 6.9 all-to-all-start.5
  724.8 7.3 convolution_bitcast_fusion
  732.1 6.3 convolution_bitcast_fusion.1
  738.4 3.9 gather_fusion
  742.9 3.6 multiply_reduce_fusion
  746.5 4.8 gather_fusion.1
  (45 shorter events, 20.4 us)
Async XLA Ops:
  7.2 58.9 %copy-start = (bf16[2,1536,256]{2,1,0:T(8,128)(2,1)S(1)}, bf16[2,1536,256]{2,1,0:T(8,128)(2,1)}, u32[]{:S(2)}) copy-start(bf16[2,1536,256]{2,1,0:T(8,128)(2,1)} %param.10) | copy-start | bytes 4718596
  7.2 236.8 %reduce-scatter.5.cloned.1.call-start = ((), (), s32[]{:S(2)}) async-start(), calls=%async_computation.9 | async-start | bytes 6684672 | tf_op jit(solution)/shard_map/reduce_scatter | solution.py:33
  65.1 1.0 copy-start.1
  71.3 0.9 copy-start.4
  71.3 314.7 %reduce-scatter.3.cloned.1.call-start = ((), (), s32[]{:S(2)}) async-start(), calls=%async_computation.8 | async-start | bytes 6684672 | tf_op jit(solution)/shard_map/reduce_scatter | solution.py:33
  123.9 1.0 copy-start.2
  534.2 145.4 %all-to-all-start.4 = ((bf16[16,128,1536]{2,1,0:T(8,128)(2,1)}), bf16[16,128,1536]{2,1,0:T(8,128)(2,1)}, u32[]{:S(2)}, u32[]{:S(2)}) async-start(bf16[16,128,1536]{2,1,0:T(8,128)(2,1)} %stack.5), calls=%async_computation.6 | async-start | bytes 12582912 | tf_op jit(solution)/shard_map/all_to_all | solution.py:12
  679.6 38.3 %all-to-all-start.2 = ((bf16[16,128,256]{2,1,0:T(8,128)(2,1)}), bf16[16,128,256]{2,1,0:T(8,128)(2,1)S(1)}, u32[]{:S(2)}, u32[]{:S(2)}) async-start(bf16[16,128,256]{2,1,0:T(8,128)(2,1)} %bitcast.81), calls=%async_computation.3 | async-start | bytes 2097152 | tf_op jit(solution)/shard_map/all_to_all | solution.py:43
  717.9 28.6 %all-to-all-start.5 = ((bf16[16,128,256]{2,1,0:T(8,128)(2,1)}), bf16[16,128,256]{2,1,0:T(8,128)(2,1)}, u32[]{:S(2)}, u32[]{:S(2)}) async-start(bf16[16,128,256]{2,1,0:T(8,128)(2,1)} %bitcast.80), calls=%async_computation.7 | async-start | bytes 2097152 | tf_op jit(solution)/shard_map/all_to_all | solution.py:43
  724.8 7.4 copy-start.3
Sparse Core Ops, SparseCore 0:
  71.4 172.5 reduce-scatter.4
  246.6 139.3 reduce-scatter.2
